TPU v7x, 32 devices: a whole 2x2x4 slice. The times are simulated.
32 devices in a mesh: comp: 8 (over y, x, core), dom: 4 (over z).
Axes of the slice: x: 2, y: 2, z: 4, core: 2. Of those that a mesh axis runs over, the one named last changes fastest.
Arguments:
- density: float32 [8, 32, 16, 16, 256], P('comp', 'dom'), may hold values from -6 to 6
- velocity: bfloat16 [8, 6, 32, 16, 16, 256], P('comp', None, 'dom'), may hold values from -0.099609375 to 0.099609375
- coefficients: int32 [8], replicated, may hold values from -1 to 1, as said below
- owner_lists: int32 [196, 8], replicated, may hold values from -1 to 255, as said below
Outputs:
- combined: float32 [8, 32, 16, 16, 256], P('comp', 'dom')
Inputs may be any that keep to these rules, and one draw needn't show every extreme that they name: `coefficients`: each is -1 or 1. `owner_lists`: every slab number c * 32 + s appears in exactly one row; within a row the entries are distinct and ascending, padding -1 follows them, and every row has at least one entry; no row names two slabs of one component; 4 rows name all 8 components; exactly 36 rows have more than one entry, and those that do not name all components have exactly two; every component has exactly 12 slabs in rows with more than one entry.
All inputs are finite; a program needn't handle non-finite values.
Results may differ from a plain program's by a relative error of at most 0.0003.
Values may be sent and summed in bfloat16 or wider, within the bound.
No kernel may reach another device: no remote copies, remote signals or barrier semaphores. Data moves between devices by JAX's collectives and lax.ppermute only.
A program may use at most 128 MiB of HBM per device.

v0:
```python
import functools

import jax
import jax.numpy as jnp
import numpy as np
from jax import lax
from jax.experimental import pallas as pl
from jax.experimental.pallas import tpu as pltpu
from jax.sharding import PartitionSpec as P

GRID_A = 32
GRID_B = 16
GRID_C = 16
LANES = 256
HALF = 128
D_STRIDE = 32
LANE_AXES = ((8, 4), (4, 1))
STEPS = 4
GROUP = 4
SHARED = 4
BORROWED = 4
MULTI = 12
LEVELS = 32000.0
FINE = 16.0
TINY = 1e-36
VMEM_LIMIT = 24 * 1024 * 1024
FIRST_LIMIT = 40 * 1024 * 1024


def params(limit=VMEM_LIMIT):
    return pltpu.CompilerParams(vmem_limit_bytes=limit)


def smem():
    return pl.BlockSpec(memory_space=pltpu.SMEM)


def hbm():
    return pl.BlockSpec(memory_space=pltpu.HBM)


def vmem():
    return pl.BlockSpec(memory_space=pltpu.VMEM)


def code_of(peak):
    return jnp.ceil(jnp.log(jnp.maximum(peak, TINY)) * (FINE / 0.6931471805599453))


def encode(rows, put, put_code):
    peak = jnp.abs(rows[0]())
    for row in rows[1:]:
        peak = jnp.maximum(peak, jnp.abs(row()))
    code = code_of(peak)
    factor = jnp.exp2(code * (-1.0 / FINE)) * LEVELS
    put_code(code.astype(jnp.int32).astype(jnp.int16))
    for index, row in enumerate(rows):
        put(index, jnp.round(row() * factor).astype(jnp.int32).astype(jnp.int16))


def to_float(block):
    return block.astype(jnp.int32).astype(jnp.float32)


def unit_of(code_row):
    return jnp.exp2(to_float(code_row) * (1.0 / FINE)) * (1.0 / LEVELS)


def message_shape():
    return jax.ShapeDtypeStruct((GRID_B + 1, GRID_C, LANES), jnp.int16)


def code_plane(read, target):
    encode(
        [lambda b=b: read(b) for b in range(GRID_B)],
        lambda b, value: target.__setitem__(b, value),
        lambda value: target.__setitem__(GRID_B, value),
    )


def code_edges(odd, grid, inner, outer):
    planes = grid.shape[0]

    def work(to_next, to_last):
        code_plane(lambda b: grid[0, b], to_last)
        code_plane(lambda b: grid[planes - 1, b], to_next)

    @pl.when(odd[0] == 0)
    def _():
        work(inner, outer)

    @pl.when(odd[0] == 1)
    def _():
        work(outer, inner)


def send_planes(grid, odd):
    return pl.pallas_call(
        lambda odd, grid, inner, outer: code_edges(odd, grid, inner, outer),
        in_specs=[smem(), vmem()],
        out_specs=[vmem()] * 2,
        out_shape=[message_shape()] * 2,
        compiler_params=params(),
    )(odd, grid)


def lane_matrix():
    point = np.arange(LANES)
    eye = np.eye(LANES)
    total = np.zeros((LANES, LANES))
    differences = []
    for extent, stride in LANE_AXES:
        place = point // stride % extent
        forward = eye[:, point + ((place + 1) % extent - place) * stride]
        backward = eye[:, point + ((place - 1) % extent - place) * stride]
        total += forward + backward
        differences.append(forward - backward)
    matrix = np.concatenate([total] + differences, 1)
    return jnp.asarray(np.concatenate([matrix, matrix], 0), jnp.bfloat16)


def lane_products(plane, matrix, products):
    value = plane.reshape(GRID_B * GRID_C, LANES)
    coarse = value.astype(jnp.bfloat16)
    fine = (value - coarse.astype(jnp.float32)).astype(jnp.bfloat16)
    products[...] = jnp.dot(
        jnp.concatenate([coarse, fine], 1), matrix[...], preferred_element_type=jnp.float32
    )


def advance(grid, matrix, speeds, out, even, odd, ready):
    planes = grid.shape[0]

    def rows(plane, products):
        up, down = jnp.minimum(plane + 1, planes - 1), jnp.maximum(plane - 1, 0)
        has_up = jnp.where(plane < planes - 1, 1.0, 0.0)
        has_down = jnp.where(plane > 0, 1.0, 0.0)
        for b in range(GRID_B):
            value = grid[plane, b]
            pairs = [
                (grid[up, b] * has_up, grid[down, b] * has_down),
                (grid[plane, (b + 1) % GRID_B], grid[plane, (b - 1) % GRID_B]),
                (pltpu.roll(value, GRID_C - 1, 0), pltpu.roll(value, 1, 0)),
                (pltpu.roll(value, LANES - D_STRIDE, 1), pltpu.roll(value, D_STRIDE, 1)),
            ]
            place = slice(b * GRID_C, (b + 1) * GRID_C)
            total = products[place, :LANES]
            drift = None
            for d in range(6):
                if d < len(pairs):
                    forward, backward = pairs[d]
                    total = total + (forward + backward)
                    difference = forward - backward
                else:
                    difference = products[place, (d - 3) * LANES : (d - 2) * LANES]
                term = speeds[d, plane, b].astype(jnp.float32) * difference
                drift = term if drift is None else drift + term
            out[plane, b] = 0.28 * value + 0.06 * total - 0.5 * drift

    lane_products(grid[0], matrix, even)

    def pair(index, carry):
        plane = 2 * index
        ready(plane)
        lane_products(grid[plane + 1], matrix, odd)
        rows(plane, even)
        ready(plane + 1)
        lane_products(grid[jnp.minimum(plane + 2, planes - 1)], matrix, even)
        rows(plane + 1, odd)
        return carry

    lax.fori_loop(0, planes // 2, pair, 0)


def advance_body(grid, matrix, speeds, out, even, odd):
    advance(grid, matrix, speeds, out, even, odd, lambda plane: None)


def first_body(grid, matrix, velocity, out, speeds, even, odd, sems):
    planes = grid.shape[0]

    def copy(plane):
        return pltpu.make_async_copy(velocity.at[0, :, plane], speeds.at[:, plane], sems.at[plane])

    for plane in range(planes):
        copy(plane).start()
    advance(grid, matrix, speeds, out, even, odd, lambda plane: copy(plane).wait())


def first_planes(grid, matrix, velocity):
    products = pltpu.VMEM((GRID_B * GRID_C, matrix.shape[1]), jnp.float32)
    return pl.pallas_call(
        first_body,
        in_specs=[vmem(), vmem(), hbm()],
        out_specs=[vmem()] * 2,
        out_shape=[
            jax.ShapeDtypeStruct(grid.shape, jnp.float32),
            jax.ShapeDtypeStruct(velocity.shape[1:], jnp.bfloat16),
        ],
        scratch_shapes=[products, products, pltpu.SemaphoreType.DMA((grid.shape[0],))],
        compiler_params=params(FIRST_LIMIT),
        cost_estimate=pl.CostEstimate(
            flops=1000 * grid.size, bytes_accessed=20 * grid.size, transcendentals=0
        ),
    )(grid, matrix, velocity)


def advance_planes(grid, matrix, velocity):
    points = grid.size
    products = pltpu.VMEM((GRID_B * GRID_C, matrix.shape[1]), jnp.float32)
    return pl.pallas_call(
        advance_body,
        in_specs=[vmem()] * 3,
        out_specs=vmem(),
        out_shape=jax.ShapeDtypeStruct(grid.shape, jnp.float32),
        scratch_shapes=[products, products],
        compiler_params=params(),
        cost_estimate=pl.CostEstimate(
            flops=1000 * points, bytes_accessed=20 * points, transcendentals=0
        ),
    )(grid, matrix, velocity)


def add_edges(odd, inner, outer, speeds, out):
    planes = out.shape[0]

    def work(from_next, from_last):
        for plane, source, sign in ((0, from_last, 0.5), (planes - 1, from_next, -0.5)):
            unit = unit_of(source[GRID_B])
            for b in range(GRID_B):
                share = 0.06 + sign * speeds[0, plane, b].astype(jnp.float32)
                out[plane, b] = out[plane, b] + to_float(source[b]) * unit * share

    @pl.when(odd[0] == 0)
    def _():
        work(inner, outer)

    @pl.when(odd[0] == 1)
    def _():
        work(outer, inner)


def edge_body(odd, partial, inner, outer, speeds, out, to_inner, to_outer):
    del partial
    add_edges(odd, inner, outer, speeds, out)
    code_edges(odd, out, to_inner, to_outer)


def edge_planes(odd, partial, inner, outer, speeds):
    return pl.pallas_call(
        edge_body,
        in_specs=[smem()] + [vmem()] * 4,
        out_specs=[vmem()] * 3,
        out_shape=[jax.ShapeDtypeStruct(partial.shape, jnp.float32)] + [message_shape()] * 2,
        input_output_aliases={1: 0},
        compiler_params=params(),
        cost_estimate=pl.CostEstimate(
            flops=2_000_000, bytes_accessed=2_000_000, transcendentals=0
        ),
    )(odd, partial, inner, outer, speeds)


class Cut:
    def __init__(self, count, planes):
        self.count, self.planes = count, planes
        self.splits = count // (2 * GRID_B)
        self.extent = GRID_C // self.splits
        self.code_rows = min(self.extent, 8)
        self.groups = self.extent // self.code_rows
        self.data_rows = planes * self.extent
        self.stack = min(planes, max(1, 16 // self.extent))
        self.per_row = 2 * self.splits

    def shape(self):
        return jax.ShapeDtypeStruct(
            (self.count, self.data_rows + self.code_rows, HALF), jnp.int16
        )

    def place(self, chunk):
        half, part = divmod(chunk, self.splits)
        return (
            slice(part * self.extent, (part + 1) * self.extent),
            slice(half * HALF, (half + 1) * HALF),
        )

    def spread(self, tile, repeats=1):
        return jnp.concatenate([tile] * (self.groups * repeats), 0)

    def put(self, target, chunk, value_of):
        peak = jnp.abs(value_of(0))
        for plane in range(1, self.planes):
            peak = jnp.maximum(peak, jnp.abs(value_of(plane)))
        top = peak[: self.code_rows]
        for group in range(1, self.groups):
            top = jnp.maximum(top, peak[group * self.code_rows : (group + 1) * self.code_rows])
        code = code_of(top)
        factor = self.spread(jnp.exp2(code * (-1.0 / FINE)) * LEVELS, self.stack)
        size = self.stack * self.extent
        for index in range(0, self.planes, self.stack):
            block = jnp.concatenate([value_of(index + i) for i in range(self.stack)], 0)
            start = index * self.extent
            target[chunk, start : start + size] = (
                jnp.round(block * factor).astype(jnp.int32).astype(jnp.int16)
            )
        target[chunk, self.data_rows :] = code.astype(jnp.int32).astype(jnp.int16)

    def values(self, source, chunk):
        unit = self.spread(unit_of(source[chunk, self.data_rows :]), self.stack)
        values = []
        size = self.stack * self.extent
        for index in range(0, self.planes, self.stack):
            start = index * self.extent
            block = to_float(source[chunk, start : start + size]) * unit
            for i in range(self.stack):
                values.append(block[i * self.extent : (i + 1) * self.extent])
        return values


def last_body(cut, odd, partial, inner, outer, speeds, grid, out):
    del partial
    add_edges(odd, inner, outer, speeds, grid)

    def pack(index, carry):
        for row in range(GROUP):
            b = index * GROUP + row
            for chunk in range(cut.per_row):
                place = cut.place(chunk)
                cut.put(out, b * cut.per_row + chunk, lambda p: grid[(p, b) + place])
        return carry

    lax.fori_loop(0, GRID_B // GROUP, pack, 0)


def last_planes(cut, odd, partial, inner, outer, speeds):
    return pl.pallas_call(
        functools.partial(last_body, cut),
        in_specs=[smem()] + [vmem()] * 4,
        out_specs=[vmem()] * 2,
        out_shape=[jax.ShapeDtypeStruct(partial.shape, jnp.float32), cut.shape()],
        input_output_aliases={1: 0},
        compiler_params=params(),
    )(odd, partial, inner, outer, speeds)


def merge_body(
    cut, dom_count, slabs, partners, weights, columns, out, values, rows, sums, grid
):
    comp_count = cut.count // dom_count

    def unpack(source, carry):
        for plane, value in enumerate(cut.values(columns, source)):
            values[source * cut.planes + plane] = value
        return carry

    lax.fori_loop(0, cut.count, unpack, 0, unroll=2)

    def gather(comp, carry):
        weight = weights[comp].astype(jnp.float32)
        base = comp * GRID_A
        for index in range(MULTI):
            slab = slabs[comp, index]
            spacing = slab & -slab
            share = jnp.where(slab > 0, -0.5 * weight, 0.0)
            near = (
                values[base + ((slab - spacing) & (GRID_A - 1))]
                + values[base + ((slab + spacing) & (GRID_A - 1))]
            )
            rows[comp * MULTI + index] = values[base + slab] * weight + near * share
        return carry

    lax.fori_loop(0, comp_count, gather, 0)
    for index in range(SHARED):
        total = rows[index]
        for comp in range(1, comp_count):
            total = total + rows[comp * MULTI + index]
        sums[index] = total
    grid[...] = jnp.zeros_like(grid)

    def scatter(comp, carry):
        for index in range(MULTI):
            if index < SHARED:
                change = sums[index] - rows[comp * MULTI + index]
            else:
                change = rows[partners[comp, index]]
            grid[comp, slabs[comp, index]] = change
        return carry

    lax.fori_loop(0, comp_count, scatter, 0)

    def send(comp, carry):
        nodal = [grid[comp, position] for position in range(GRID_A)]
        spacing = GRID_A // 2
        while spacing >= 1:
            for position in range(spacing, GRID_A, 2 * spacing):
                nodal[position] = nodal[position] + 0.5 * (
                    nodal[position - spacing] + nodal[(position + spacing) % GRID_A]
                )
            spacing //= 2
        for dom in range(dom_count):
            cut.put(out, comp * dom_count + dom, lambda p: nodal[dom * cut.planes + p])
        return carry

    lax.fori_loop(0, comp_count, send, 0)


def merge_columns(cut, columns, slabs, partners, weights, dom_count):
    comp_count = cut.count // dom_count
    tile = (cut.extent, HALF)
    return pl.pallas_call(
        functools.partial(merge_body, cut, dom_count),
        in_specs=[smem()] * 3 + [vmem()],
        out_specs=vmem(),
        out_shape=cut.shape(),
        scratch_shapes=[
            pltpu.VMEM((comp_count * GRID_A,) + tile, jnp.float32),
            pltpu.VMEM((comp_count * MULTI,) + tile, jnp.float32),
            pltpu.VMEM((SHARED,) + tile, jnp.float32),
            pltpu.VMEM((comp_count, GRID_A) + tile, jnp.float32),
        ],
        compiler_params=params(),
    )(slabs, partners, weights, columns)


def final_body(cut, weights, comp, grid, changes, out, stage, sems):
    weight = weights[comp[0]].astype(jnp.float32)

    def copy(index):
        span = pl.ds(index * GROUP, GROUP)
        return pltpu.make_async_copy(stage.at[:, span], out.at[0, :, span], sems.at[index])

    def combine(index, carry):
        for row in range(GROUP):
            b = index * GROUP + row
            for chunk in range(cut.per_row):
                place = cut.place(chunk)
                for p, value in enumerate(cut.values(changes, b * cut.per_row + chunk)):
                    stage[(p, b) + place] = grid[(p, b) + place] * weight + value
        copy(index).start()
        return carry

    lax.fori_loop(0, GRID_B // GROUP, combine, 0)
    for index in range(GRID_B // GROUP):
        copy(index).wait()


def final_planes(cut, grid, changes, weights, comp):
    return pl.pallas_call(
        functools.partial(final_body, cut),
        in_specs=[smem(), smem(), vmem(), vmem()],
        out_specs=hbm(),
        out_shape=jax.ShapeDtypeStruct((1,) + grid.shape, jnp.float32),
        scratch_shapes=[
            pltpu.VMEM(grid.shape, jnp.float32),
            pltpu.SemaphoreType.DMA((GRID_B // GROUP,)),
        ],
        compiler_params=params(),
    )(weights, comp, grid, changes)


def tables_body(owners, slabs, partners, places):
    blocks = owners.shape[0]
    comp_count = slabs.shape[0]

    def clear(comp, carry):
        places[comp] = SHARED
        for index in range(SHARED):
            partners[comp, index] = 0
        return carry

    lax.fori_loop(0, comp_count, clear, 0)

    def block(number, shared):
        first, second = owners[number, 0], owners[number, 1]
        is_shared = owners[number, 2] >= 0

        @pl.when((second >= 0) & ~is_shared)
        def _():
            comps = [lax.div(slab, GRID_A) for slab in (first, second)]
            own = [places[comp] for comp in comps]
            for side, slab in enumerate((first, second)):
                slabs[comps[side], own[side]] = lax.rem(slab, GRID_A)
                partners[comps[side], own[side]] = comps[1 - side] * MULTI + own[1 - side]
                places[comps[side]] = own[side] + 1

        @pl.when(is_shared)
        def _():
            def holder(index, carry):
                slab = owners[number, index]
                slabs[lax.div(slab, GRID_A), shared] = lax.rem(slab, GRID_A)
                return carry

            lax.fori_loop(0, comp_count, holder, 0)

        return shared + jnp.where(is_shared, 1, 0)

    lax.fori_loop(0, blocks, block, 0)


def merge_tables(owner_lists, comp_count):
    shape = jax.ShapeDtypeStruct((comp_count, MULTI), jnp.int32)
    return pl.pallas_call(
        tables_body,
        in_specs=[smem()],
        out_specs=[smem()] * 2,
        out_shape=[shape] * 2,
        scratch_shapes=[pltpu.SMEM((comp_count,), jnp.int32)],
    )(owner_lists)


def local(density, velocity, coefficients, owner_lists):
    comp_count, dom_count = lax.axis_size("comp"), lax.axis_size("dom")
    inner_pairs = [(i, i ^ 1) for i in range(dom_count)]
    outer_pairs = [(i, (i - 1 + 2 * (i % 2)) % dom_count) for i in range(dom_count)]

    matrix = lane_matrix()
    odd = (lax.axis_index("dom") % 2).astype(jnp.int32).reshape(1)
    comp = lax.axis_index("comp").astype(jnp.int32).reshape(1)
    grid = density[0]
    to_inner, to_outer = send_planes(grid, odd)
    for step in range(STEPS):
        inner = lax.ppermute(to_inner, "dom", inner_pairs)
        outer = lax.ppermute(to_outer, "dom", outer_pairs)
        if step == 0:
            partial, speeds = first_planes(grid, matrix, velocity)
        else:
            partial = advance_planes(grid, matrix, speeds)
        if step < STEPS - 1:
            grid, to_inner, to_outer = edge_planes(odd, partial, inner, outer, speeds)
    cut = Cut(comp_count * dom_count, density.shape[1])
    grid, columns = last_planes(cut, odd, partial, inner, outer, speeds)
    columns, owner_lists = lax.optimization_barrier((columns, owner_lists))
    columns = lax.all_to_all(columns, ("comp", "dom"), 0, 0, tiled=True)
    slabs, partners = merge_tables(owner_lists, comp_count)
    changes = merge_columns(cut, columns, slabs, partners, coefficients, dom_count)
    changes = lax.all_to_all(changes, ("comp", "dom"), 0, 0, tiled=True)
    return final_planes(cut, grid, changes, coefficients, comp)


def solution(mesh):
    in_specs = (
        P("comp", "dom", None, None, None),
        P("comp", None, "dom", None, None, None),
        P(),
        P(),
    )
    out_specs = P("comp", "dom", None, None, None)
    return jax.shard_map(local, mesh=mesh, in_specs=in_specs, out_specs=out_specs, check_vma=False)
```

profile of v0, /device:TPU:1, one launch (start us, length us, event | category | flops | bytes accessed | tf_op | source)
XLA Modules:
  0.0 110.9 jit_solution(15307585599963057826)
XLA Ops:
  0.0 0.0 copy-start
  0.0 0.0 copy-start.1
  0.0 1.7 %copy-done.1 = f32[1,8,16,16,256]{4,3,2,1,0:T(8,128)S(1)} copy-done((f32[1,8,16,16,256]{4,3,2,1,0:T(8,128)S(1)}, f32[1,8,16,16,256]{4,3,2,1,0:T(8,128)}, u32[]{:S(2)}) %copy-start.1) | copy-done | bytes 2097176
  1.7 0.1 shard_map.56
  1.8 2.2 %collective-permute-start = (s16[17,16,256]{2,1,0:T(8,128)(2,1)S(1)}, s16[17,16,256]{2,1,0:T(8,128)(2,1)S(1)}, u32[]{:S(2)}, u32[]{:S(2)}) collective-permute-start(s16[17,16,256]{2,1,0:T(8,128)(2,1)S(1)} %get-tuple-element.25), channel_id=1, source_target_pairs={{0,1},{1,0},{2,3},{3,2},{4,5},{5,4},{6,7},{7,6},{8,9},{9,8},{10,11... | collective-permute-start | bytes 417800 | tf_op jit(solution)/shard_map/ppermute | solution.py:521
  4.0 2.2 %collective-permute-start.1 = (s16[17,16,256]{2,1,0:T(8,128)(2,1)S(1)}, s16[17,16,256]{2,1,0:T(8,128)(2,1)S(1)}, u32[]{:S(2)}, u32[]{:S(2)}) collective-permute-start(s16[17,16,256]{2,1,0:T(8,128)(2,1)S(1)} %get-tuple-element.26), channel_id=1, source_target_pairs={{0,3},{1,2},{2,1},{3,0},{4,7},{5,6},{6,5},{7,4},{8,11},{9,10},{10,... | collective-permute-start | bytes 417800 | tf_op jit(solution)/shard_map/ppermute | solution.py:522
  6.2 0.0 copy-done
  6.2 0.0 copy-start.2
  6.2 1.6 %copy-done.2 = f32[1,8,16,16,256]{4,3,2,1,0:T(8,128)S(1)} copy-done((f32[1,8,16,16,256]{4,3,2,1,0:T(8,128)S(1)}, f32[1,8,16,16,256]{4,3,2,1,0:T(8,128)}, u32[]{:S(2)}) %copy-start.2) | copy-done | bytes 2097176
  7.8 5.9 %shard_map.55 = (f32[8,16,16,256]{3,2,1,0:T(8,128)S(1)}, bf16[6,8,16,16,256]{4,3,2,1,0:T(8,128)(2,1)S(1)}) custom-call(f32[8,16,16,256]{3,2,1,0:T(8,128)S(1)} %bitcast.4, bf16[512,768]{1,0:T(8,128)(2,1)S(1)} %copy-done, bf16[1,6,8,16,16,256]{5,4,3,2,1,0:T(8,128)(2,1)} %velocity.1), custom_call_target="tpu_custom_call" | custom-call | flops 524288000 | bytes 10485760 | tf_op jit(solution)/shard_map/pallas_call | solution.py:192
  13.7 0.0 collective-permute-done.inner
  13.7 0.0 collective-permute-done.1.outer
  13.7 0.3 shard_map.57
  13.9 0.5 collective-permute-start.2
  14.4 0.9 collective-permute-start.3
  15.3 4.3 %shard_map.58.partial = f32[8,16,16,256]{3,2,1,0:T(8,128)S(1)} custom-call(f32[8,16,16,256]{3,2,1,0:T(8,128)S(1)} %get-tuple-element.28.grid, bf16[512,768]{1,0:T(8,128)(2,1)S(1)} %copy-done, bf16[6,8,16,16,256]{4,3,2,1,0:T(8,128)(2,1)S(1)} %get-tuple-element.27.speeds), custom_call_target="tpu_custom_call" | custom-call | flops 524288000 | bytes 10485760 | tf_op jit(solution)/shard_map/pallas_call | solution.py:211
  19.6 0.0 collective-permute-done.2.inner
  19.6 2.2 %collective-permute-done.3.outer = s16[17,16,256]{2,1,0:T(8,128)(2,1)S(1)} collective-permute-done((s16[17,16,256]{2,1,0:T(8,128)(2,1)S(1)}, s16[17,16,256]{2,1,0:T(8,128)(2,1)S(1)}, u32[]{:S(2)}, u32[]{:S(2)}) %collective-permute-start.3) | collective-permute-done | bytes 139296 | tf_op jit(solution)/shard_map/ppermute | solution.py:522
  21.8 0.3 shard_map.59
  22.1 0.1 collective-permute-start.4
  22.2 1.1 collective-permute-start.5
  23.2 4.3 %shard_map.60.partial = f32[8,16,16,256]{3,2,1,0:T(8,128)S(1)} custom-call(f32[8,16,16,256]{3,2,1,0:T(8,128)S(1)} %get-tuple-element.31.grid, bf16[512,768]{1,0:T(8,128)(2,1)S(1)} %copy-done, bf16[6,8,16,16,256]{4,3,2,1,0:T(8,128)(2,1)S(1)} %get-tuple-element.27.speeds), custom_call_target="tpu_custom_call" | custom-call | flops 524288000 | bytes 10485760 | tf_op jit(solution)/shard_map/pallas_call | solution.py:211
  27.5 0.0 collective-permute-done.4.inner
  27.6 0.9 collective-permute-done.5.outer
  28.5 0.3 shard_map.61
  28.8 1.2 %collective-permute-start.6 = (s16[17,16,256]{2,1,0:T(8,128)(2,1)S(1)}, s16[17,16,256]{2,1,0:T(8,128)(2,1)S(1)}, u32[]{:S(2)}, u32[]{:S(2)}) collective-permute-start(s16[17,16,256]{2,1,0:T(8,128)(2,1)S(1)} %get-tuple-element.35), channel_id=1, source_target_pairs={{0,1},{1,0},{2,3},{3,2},{4,5},{5,4},{6,7},{7,6},{8,9},{9,8},{10,11... | collective-permute-start | bytes 417800 | tf_op jit(solution)/shard_map/ppermute | solution.py:521
  29.9 0.7 collective-permute-start.7
  30.7 4.3 %shard_map.62.partial = f32[8,16,16,256]{3,2,1,0:T(8,128)S(1)} custom-call(f32[8,16,16,256]{3,2,1,0:T(8,128)S(1)} %get-tuple-element.34.grid, bf16[512,768]{1,0:T(8,128)(2,1)S(1)} %copy-done, bf16[6,8,16,16,256]{4,3,2,1,0:T(8,128)(2,1)S(1)} %get-tuple-element.27.speeds), custom_call_target="tpu_custom_call" | custom-call | flops 524288000 | bytes 10485760 | tf_op jit(solution)/shard_map/pallas_call | solution.py:211
  35.0 0.0 collective-permute-done.6.inner
  35.0 0.7 collective-permute-done.7.outer
  35.7 0.5 shard_map.63
  36.2 0.0 copy-start.4
  36.2 1.0 copy-done.4
  37.2 0.0 copy-start.8
  37.2 8.1 %all-to-all-start = ((s16[32,136,128]{2,1,0:T(8,128)(2,1)}), s16[32,136,128]{2,1,0:T(8,128)(2,1)S(1)}, u32[]{:S(2)}, u32[]{:S(2)}) async-start(s16[32,136,128]{2,1,0:T(8,128)(2,1)} %copy-done.4), calls=%async_computation | async-start | bytes 2228224 | tf_op jit(solution)/shard_map/all_to_all | solution.py:532
  45.3 0.0 copy-done.8
  45.3 0.8 copy.10.owners
  46.1 9.3 %shard_map.64 = (s32[8,12]{1,0:T(8,128)}, s32[8,12]{1,0:T(8,128)}) custom-call(s32[196,8]{1,0:T(8,128)} %copy.10.owners), custom_call_target="tpu_custom_call" | custom-call | tf_op jit(solution)/shard_map/pallas_call | solution.py:501
  55.4 17.7 %all-to-all-done.columns = s16[32,136,128]{2,1,0:T(8,128)(2,1)S(1)} async-done(((s16[32,136,128]{2,1,0:T(8,128)(2,1)}), s16[32,136,128]{2,1,0:T(8,128)(2,1)S(1)}, u32[]{:S(2)}, u32[]{:S(2)}) %all-to-all-start) | async-done | bytes 1114144 | tf_op jit(solution)/shard_map/all_to_all | solution.py:532
  73.1 0.0 copy-done.7
  73.1 0.7 copy-done.5
  73.8 0.7 copy-done.6
  74.4 2.6 %shard_map.65 = s16[32,136,128]{2,1,0:T(8,128)(2,1)S(1)} custom-call(s32[8,12]{1,0:T(8,128)S(1)} %copy-done.5, s32[8,12]{1,0:T(8,128)S(1)} %copy-done.6, s32[8]{0:T(128)S(1)} %copy-done.7, s16[32,136,128]{2,1,0:T(8,128)(2,1)S(1)} %all-to-all-done.columns), custom_call_target="tpu_custom_call" | custom-call | tf_op jit(solution)/shard_map/pallas_call | solution.py:409
  77.0 0.0 copy-start.3
  77.0 1.0 copy-done.3
  78.0 3.2 %all-to-all-start.1 = ((s16[32,136,128]{2,1,0:T(8,128)(2,1)}), s16[32,136,128]{2,1,0:T(8,128)(2,1)S(1)}, u32[]{:S(2)}, u32[]{:S(2)}) async-start(s16[32,136,128]{2,1,0:T(8,128)(2,1)} %copy-done.3), calls=%async_computation.1 | async-start | bytes 2228224 | tf_op jit(solution)/shard_map/all_to_all | solution.py:535
  81.2 27.7 %all-to-all-done.1.changes = s16[32,136,128]{2,1,0:T(8,128)(2,1)S(1)} async-done(((s16[32,136,128]{2,1,0:T(8,128)(2,1)}), s16[32,136,128]{2,1,0:T(8,128)(2,1)S(1)}, u32[]{:S(2)}, u32[]{:S(2)}) %all-to-all-start.1) | async-done | bytes 1114144 | tf_op jit(solution)/shard_map/all_to_all | solution.py:535
  108.9 2.0 %shard_map.66 = f32[1,8,16,16,256]{4,3,2,1,0:T(8,128)} custom-call(s32[8]{0:T(128)S(1)} %copy-done.7, s32[1]{0:T(128)} %bitcast.comp, f32[8,16,16,256]{3,2,1,0:T(8,128)S(1)} %get-tuple-element.37.grid, s16[32,136,128]{2,1,0:T(8,128)(2,1)S(1)} %all-to-all-done.1.changes), custom_call_target="tpu_custom_call" | custom-call | tf_op jit(solution)/shard_map/pallas_call | solution.py:447
  (3 shorter events, 0.0 us)
Async XLA Ops:
  0.0 6.2 %copy-start = (bf16[512,768]{1,0:T(8,128)(2,1)S(1)}, bf16[512,768]{1,0:T(8,128)(2,1)}, u32[]{:S(2)}) copy-start(bf16[512,768]{1,0:T(8,128)(2,1)} %constant.24.clone.matrix) | copy-start | bytes 2359300
  0.0 1.7 %copy-start.1 = (f32[1,8,16,16,256]{4,3,2,1,0:T(8,128)S(1)}, f32[1,8,16,16,256]{4,3,2,1,0:T(8,128)}, u32[]{:S(2)}) copy-start(f32[1,8,16,16,256]{4,3,2,1,0:T(8,128)} %param.5) | copy-start | bytes 6291460
  1.8 11.9 %collective-permute-start = (s16[17,16,256]{2,1,0:T(8,128)(2,1)S(1)}, s16[17,16,256]{2,1,0:T(8,128)(2,1)S(1)}, u32[]{:S(2)}, u32[]{:S(2)}) collective-permute-start(s16[17,16,256]{2,1,0:T(8,128)(2,1)S(1)} %get-tuple-element.25), channel_id=1, source_target_pairs={{0,1},{1,0},{2,3},{3,2},{4,5},{5,4},{6,7},{7,6},{8,9},{9,8},{10,11... | collective-permute-start | bytes 417800 | tf_op jit(solution)/shard_map/ppermute | solution.py:521
  4.0 9.7 %collective-permute-start.1 = (s16[17,16,256]{2,1,0:T(8,128)(2,1)S(1)}, s16[17,16,256]{2,1,0:T(8,128)(2,1)S(1)}, u32[]{:S(2)}, u32[]{:S(2)}) collective-permute-start(s16[17,16,256]{2,1,0:T(8,128)(2,1)S(1)} %get-tuple-element.26), channel_id=1, source_target_pairs={{0,3},{1,2},{2,1},{3,0},{4,7},{5,6},{6,5},{7,4},{8,11},{9,10},{10,... | collective-permute-start | bytes 417800 | tf_op jit(solution)/shard_map/ppermute | solution.py:522
  6.2 1.6 %copy-start.2 = (f32[1,8,16,16,256]{4,3,2,1,0:T(8,128)S(1)}, f32[1,8,16,16,256]{4,3,2,1,0:T(8,128)}, u32[]{:S(2)}) copy-start(f32[1,8,16,16,256]{4,3,2,1,0:T(8,128)} %param.5) | copy-start | bytes 6291460
  13.9 5.7 %collective-permute-start.2 = (s16[17,16,256]{2,1,0:T(8,128)(2,1)S(1)}, s16[17,16,256]{2,1,0:T(8,128)(2,1)S(1)}, u32[]{:S(2)}, u32[]{:S(2)}) collective-permute-start(s16[17,16,256]{2,1,0:T(8,128)(2,1)S(1)} %get-tuple-element.29), channel_id=1, source_target_pairs={{0,1},{1,0},{2,3},{3,2},{4,5},{5,4},{6,7},{7,6},{8,9},{9,8},{10,11... | collective-permute-start | bytes 417800 | tf_op jit(solution)/shard_map/ppermute | solution.py:521
  14.4 7.4 %collective-permute-start.3 = (s16[17,16,256]{2,1,0:T(8,128)(2,1)S(1)}, s16[17,16,256]{2,1,0:T(8,128)(2,1)S(1)}, u32[]{:S(2)}, u32[]{:S(2)}) collective-permute-start(s16[17,16,256]{2,1,0:T(8,128)(2,1)S(1)} %get-tuple-element.30), channel_id=1, source_target_pairs={{0,3},{1,2},{2,1},{3,0},{4,7},{5,6},{6,5},{7,4},{8,11},{9,10},{10,... | collective-permute-start | bytes 417800 | tf_op jit(solution)/shard_map/ppermute | solution.py:522
  22.1 5.5 %collective-permute-start.4 = (s16[17,16,256]{2,1,0:T(8,128)(2,1)S(1)}, s16[17,16,256]{2,1,0:T(8,128)(2,1)S(1)}, u32[]{:S(2)}, u32[]{:S(2)}) collective-permute-start(s16[17,16,256]{2,1,0:T(8,128)(2,1)S(1)} %get-tuple-element.32), channel_id=1, source_target_pairs={{0,1},{1,0},{2,3},{3,2},{4,5},{5,4},{6,7},{7,6},{8,9},{9,8},{10,11... | collective-permute-start | bytes 417800 | tf_op jit(solution)/shard_map/ppermute | solution.py:521
  22.2 6.3 %collective-permute-start.5 = (s16[17,16,256]{2,1,0:T(8,128)(2,1)S(1)}, s16[17,16,256]{2,1,0:T(8,128)(2,1)S(1)}, u32[]{:S(2)}, u32[]{:S(2)}) collective-permute-start(s16[17,16,256]{2,1,0:T(8,128)(2,1)S(1)} %get-tuple-element.33), channel_id=1, source_target_pairs={{0,3},{1,2},{2,1},{3,0},{4,7},{5,6},{6,5},{7,4},{8,11},{9,10},{10,... | collective-permute-start | bytes 417800 | tf_op jit(solution)/shard_map/ppermute | solution.py:522
  28.8 6.2 %collective-permute-start.6 = (s16[17,16,256]{2,1,0:T(8,128)(2,1)S(1)}, s16[17,16,256]{2,1,0:T(8,128)(2,1)S(1)}, u32[]{:S(2)}, u32[]{:S(2)}) collective-permute-start(s16[17,16,256]{2,1,0:T(8,128)(2,1)S(1)} %get-tuple-element.35), channel_id=1, source_target_pairs={{0,1},{1,0},{2,3},{3,2},{4,5},{5,4},{6,7},{7,6},{8,9},{9,8},{10,11... | collective-permute-start | bytes 417800 | tf_op jit(solution)/shard_map/ppermute | solution.py:521
  29.9 5.7 %collective-permute-start.7 = (s16[17,16,256]{2,1,0:T(8,128)(2,1)S(1)}, s16[17,16,256]{2,1,0:T(8,128)(2,1)S(1)}, u32[]{:S(2)}, u32[]{:S(2)}) collective-permute-start(s16[17,16,256]{2,1,0:T(8,128)(2,1)S(1)} %get-tuple-element.36), channel_id=1, source_target_pairs={{0,3},{1,2},{2,1},{3,0},{4,7},{5,6},{6,5},{7,4},{8,11},{9,10},{10,... | collective-permute-start | bytes 417800 | tf_op jit(solution)/shard_map/ppermute | solution.py:522
  36.2 1.0 copy-start.4
  37.2 8.1 %copy-start.8 = (s32[196,8]{0,1:T(8,128)S(1)}, s32[196,8]{0,1:T(8,128)}, u32[]{:S(2)}) copy-start(s32[196,8]{0,1:T(8,128)} %param.8) | copy-start | bytes 18820
  37.2 35.8 %copy-start.7 = (s32[8]{0:T(128)S(1)}, s32[8]{0:T(128)}, u32[]{:S(2)}) copy-start(s32[8]{0:T(128)} %weights.3) | copy-start | bytes 100
  37.2 35.8 %all-to-all-start = ((s16[32,136,128]{2,1,0:T(8,128)(2,1)}), s16[32,136,128]{2,1,0:T(8,128)(2,1)S(1)}, u32[]{:S(2)}, u32[]{:S(2)}) async-start(s16[32,136,128]{2,1,0:T(8,128)(2,1)} %copy-done.4), calls=%async_computation | async-start | bytes 2228224 | tf_op jit(solution)/shard_map/all_to_all | solution.py:532
  73.1 0.7 copy-start.5
  73.8 0.7 copy-start.6
  77.0 1.0 copy-start.3
  78.0 30.9 %all-to-all-start.1 = ((s16[32,136,128]{2,1,0:T(8,128)(2,1)}), s16[32,136,128]{2,1,0:T(8,128)(2,1)S(1)}, u32[]{:S(2)}, u32[]{:S(2)}) async-start(s16[32,136,128]{2,1,0:T(8,128)(2,1)} %copy-done.3), calls=%async_computation.1 | async-start | bytes 2228224 | tf_op jit(solution)/shard_map/all_to_all | solution.py:535
where the time goes:
time: 111 us
  waiting for transfers between devices  49.3 us (44%)
  Pallas kernels  34 us (31%)
  starting transfers between devices  20 us (18%)
  local copies, waits for them, and re-layouts  7.35 us (7%)
    all_to_all x1, waiting for transfers between devices, local(): changes = lax.all_to_all(changes, ('comp', 'dom'), 0, 0, tiled=True)  27.7 us
    all_to_all x1, waiting for transfers between devices, local(): columns = lax.all_to_all(columns, ('comp', 'dom'), 0, 0, tiled=True)  17.7 us
    pallas_call x3, Pallas kernels, advance_planes(): pl.pallas_call(advance_body, in_specs=[vmem()] * 3, out_specs=vmem(), out...  12.9 us
    pallas_call x1, Pallas kernels, merge_tables(): pl.pallas_call(tables_body, in_specs=[smem()], out_specs=[smem()] * 2, ou...  9.31 us
    all_to_all x1, starting transfers between devices, local(): columns = lax.all_to_all(columns, ('comp', 'dom'), 0, 0, tiled=True)  8.09 us
    unnamed x18, local copies, waits for them, and re-layouts  6.6 us
    pallas_call x1, Pallas kernels, first_planes(): pl.pallas_call(first_body, in_specs=[vmem(), vmem(), hbm()], out_specs=[v...  5.9 us
    ppermute x4, starting transfers between devices, local(): outer = lax.ppermute(to_outer, 'dom', outer_pairs)  4.9 us
  transfers between devices with their start and end apart: 10, of which 5 were waited for; matrix products, arithmetic and copies ran while one was open for 1% of the time, Pallas kernels for 25%

commit v1 on v0

--- a/solution.py
+++ b/solution.py
@@ -94,12 +94,18 @@
         work(outer, inner)
 
 
+def send_planes_body(odd, density, inner, outer, grid):
+    del density
+    code_edges(odd, grid, inner, outer)
+
+
 def send_planes(grid, odd):
     return pl.pallas_call(
-        lambda odd, grid, inner, outer: code_edges(odd, grid, inner, outer),
+        send_planes_body,
         in_specs=[smem(), vmem()],
-        out_specs=[vmem()] * 2,
-        out_shape=[message_shape()] * 2,
+        out_specs=[vmem()] * 3,
+        out_shape=[message_shape()] * 2 + [jax.ShapeDtypeStruct(grid.shape, jnp.float32)],
+        input_output_aliases={1: 2},
         compiler_params=params(),
     )(odd, grid)
 
@@ -343,7 +349,7 @@
 
 
 def merge_body(
-    cut, dom_count, slabs, partners, weights, columns, out, values, rows, sums, grid
+    cut, dom_count, table, weights, columns, out, values, rows, sums, grid
 ):
     comp_count = cut.count // dom_count
 
@@ -358,7 +364,7 @@
         weight = weights[comp].astype(jnp.float32)
         base = comp * GRID_A
         for index in range(MULTI):
-            slab = slabs[comp, index]
+            slab = table[comp, index]
             spacing = slab & -slab
             share = jnp.where(slab > 0, -0.5 * weight, 0.0)
             near = (
@@ -381,8 +387,8 @@
             if index < SHARED:
                 change = sums[index] - rows[comp * MULTI + index]
             else:
-                change = rows[partners[comp, index]]
-            grid[comp, slabs[comp, index]] = change
+                change = rows[table[comp, MULTI + index]]
+            grid[comp, table[comp, index]] = change
         return carry
 
     lax.fori_loop(0, comp_count, scatter, 0)
@@ -403,12 +409,12 @@
     lax.fori_loop(0, comp_count, send, 0)
 
 
-def merge_columns(cut, columns, slabs, partners, weights, dom_count):
+def merge_columns(cut, columns, table, weights, dom_count):
     comp_count = cut.count // dom_count
     tile = (cut.extent, HALF)
     return pl.pallas_call(
         functools.partial(merge_body, cut, dom_count),
-        in_specs=[smem()] * 3 + [vmem()],
+        in_specs=[smem()] * 2 + [vmem()],
         out_specs=vmem(),
         out_shape=cut.shape(),
         scratch_shapes=[
@@ -418,12 +424,10 @@
             pltpu.VMEM((comp_count, GRID_A) + tile, jnp.float32),
         ],
         compiler_params=params(),
-    )(slabs, partners, weights, columns)
-
-
-def final_body(cut, weights, comp, grid, changes, out, stage, sems):
-    weight = weights[comp[0]].astype(jnp.float32)
-
+    )(table, weights, columns)
+
+
+def final_body(cut, weight, grid, changes, out, stage, sems):
     def copy(index):
         span = pl.ds(index * GROUP, GROUP)
         return pltpu.make_async_copy(stage.at[:, span], out.at[0, :, span], sems.at[index])
@@ -434,7 +438,7 @@
             for chunk in range(cut.per_row):
                 place = cut.place(chunk)
                 for p, value in enumerate(cut.values(changes, b * cut.per_row + chunk)):
-                    stage[(p, b) + place] = grid[(p, b) + place] * weight + value
+                    stage[(p, b) + place] = grid[(p, b) + place] * weight[0] + value
         copy(index).start()
         return carry
 
@@ -443,10 +447,10 @@
         copy(index).wait()
 
 
-def final_planes(cut, grid, changes, weights, comp):
+def final_planes(cut, grid, changes, weight):
     return pl.pallas_call(
         functools.partial(final_body, cut),
-        in_specs=[smem(), smem(), vmem(), vmem()],
+        in_specs=[smem(), vmem(), vmem()],
         out_specs=hbm(),
         out_shape=jax.ShapeDtypeStruct((1,) + grid.shape, jnp.float32),
         scratch_shapes=[
@@ -454,17 +458,17 @@
             pltpu.SemaphoreType.DMA((GRID_B // GROUP,)),
         ],
         compiler_params=params(),
-    )(weights, comp, grid, changes)
-
-
-def tables_body(owners, slabs, partners, places):
+    )(weight, grid, changes)
+
+
+def tables_body(owners, table, places):
     blocks = owners.shape[0]
-    comp_count = slabs.shape[0]
+    comp_count = table.shape[0]
 
     def clear(comp, carry):
         places[comp] = SHARED
         for index in range(SHARED):
-            partners[comp, index] = 0
+            table[comp, MULTI + index] = 0
         return carry
 
     lax.fori_loop(0, comp_count, clear, 0)
@@ -478,15 +482,16 @@
             comps = [lax.div(slab, GRID_A) for slab in (first, second)]
             own = [places[comp] for comp in comps]
             for side, slab in enumerate((first, second)):
-                slabs[comps[side], own[side]] = lax.rem(slab, GRID_A)
-                partners[comps[side], own[side]] = comps[1 - side] * MULTI + own[1 - side]
+                table[comps[side], own[side]] = lax.rem(slab, GRID_A)
+                partner = comps[1 - side] * MULTI + own[1 - side]
+                table[comps[side], MULTI + own[side]] = partner
                 places[comps[side]] = own[side] + 1
 
         @pl.when(is_shared)
         def _():
             def holder(index, carry):
                 slab = owners[number, index]
-                slabs[lax.div(slab, GRID_A), shared] = lax.rem(slab, GRID_A)
+                table[lax.div(slab, GRID_A), shared] = lax.rem(slab, GRID_A)
                 return carry
 
             lax.fori_loop(0, comp_count, holder, 0)
@@ -497,12 +502,11 @@
 
 
 def merge_tables(owner_lists, comp_count):
-    shape = jax.ShapeDtypeStruct((comp_count, MULTI), jnp.int32)
     return pl.pallas_call(
         tables_body,
         in_specs=[smem()],
-        out_specs=[smem()] * 2,
-        out_shape=[shape] * 2,
+        out_specs=smem(),
+        out_shape=jax.ShapeDtypeStruct((comp_count, 2 * MULTI), jnp.int32),
         scratch_shapes=[pltpu.SMEM((comp_count,), jnp.int32)],
     )(owner_lists)
 
@@ -514,9 +518,7 @@
 
     matrix = lane_matrix()
     odd = (lax.axis_index("dom") % 2).astype(jnp.int32).reshape(1)
-    comp = lax.axis_index("comp").astype(jnp.int32).reshape(1)
-    grid = density[0]
-    to_inner, to_outer = send_planes(grid, odd)
+    to_inner, to_outer, grid = send_planes(density[0], odd)
     for step in range(STEPS):
         inner = lax.ppermute(to_inner, "dom", inner_pairs)
         outer = lax.ppermute(to_outer, "dom", outer_pairs)
@@ -530,10 +532,12 @@
     grid, columns = last_planes(cut, odd, partial, inner, outer, speeds)
     columns, owner_lists = lax.optimization_barrier((columns, owner_lists))
     columns = lax.all_to_all(columns, ("comp", "dom"), 0, 0, tiled=True)
-    slabs, partners = merge_tables(owner_lists, comp_count)
-    changes = merge_columns(cut, columns, slabs, partners, coefficients, dom_count)
+    table = merge_tables(owner_lists, comp_count)
+    changes = merge_columns(cut, columns, table, coefficients, dom_count)
+    changes, coefficients = lax.optimization_barrier((changes, coefficients))
+    weight = lax.dynamic_slice_in_dim(coefficients, lax.axis_index("comp"), 1).astype(jnp.float32)
     changes = lax.all_to_all(changes, ("comp", "dom"), 0, 0, tiled=True)
-    return final_planes(cut, grid, changes, coefficients, comp)
+    return final_planes(cut, grid, changes, weight)
 
 
 def solution(mesh):

time: 111 us -> 109 us (0.982)
  waiting for transfers between devices: 49.3 us -> 44.3 us
  starting transfers between devices: 20 us -> 24.3 us
  local copies, waits for them, and re-layouts: 7.35 us -> 4.65 us
    ppermute x4, starting transfers between devices: 4.9 us -> 9.87 us  [local(): outer = lax.ppermute(to_outer, 'dom', outer_pairs)]
    unnamed x18 -> x11, local copies, waits for them, and re-layouts: 6.6 us -> 3.27 us
    ppermute x4, waiting for transfers between devices: 3.86 us -> 0.66 us  [local(): outer = lax.ppermute(to_outer, 'dom', outer_pairs)]
    all_to_all x1, waiting for transfers between devices: 27.7 us -> 26.5 us  [local(): changes = lax.all_to_all(changes, ('comp', 'dom'), 0, 0, tiled=True)]
  transfers between devices with their start and end apart: 10 -> 10, of which waited for: 5 -> 4; matrix products, arithmetic and copies ran while one was open for 1% -> 1% of each run, Pallas kernels for 25% -> 26%
where the time goes in v1:
time: 109 us
  waiting for transfers between devices  44.3 us (41%)
  Pallas kernels  35 us (32%)
  starting transfers between devices  24.3 us (22%)
  local copies, waits for them, and re-layouts  4.65 us (4%)
    all_to_all x1, waiting for transfers between devices, local(): changes = lax.all_to_all(changes, ('comp', 'dom'), 0, 0, tiled=True)  26.5 us
    all_to_all x1, waiting for transfers between devices, local(): columns = lax.all_to_all(columns, ('comp', 'dom'), 0, 0, tiled=True)  17.1 us
    pallas_call x3, Pallas kernels, advance_planes(): pl.pallas_call(advance_body, in_specs=[vmem()] * 3, out_specs=vmem(), out...  12.9 us
    ppermute x4, starting transfers between devices, local(): outer = lax.ppermute(to_outer, 'dom', outer_pairs)  9.87 us
    pallas_call x1, Pallas kernels, merge_tables(): pl.pallas_call(tables_body, in_specs=[smem()], out_specs=smem(), out_shap...  9.86 us
    all_to_all x1, starting transfers between devices, local(): columns = lax.all_to_all(columns, ('comp', 'dom'), 0, 0, tiled=True)  8.15 us
    pallas_call x1, Pallas kernels, first_planes(): pl.pallas_call(first_body, in_specs=[vmem(), vmem(), hbm()], out_specs=[v...  5.9 us
    pallas_call x1, Pallas kernels, merge_columns(): pl.pallas_call(functools.partial(merge_body, cut, dom_count), in_specs=[s...  3.5 us
  transfers between devices with their start and end apart: 10, of which 4 were waited for; matrix products, arithmetic and copies ran while one was open for 1% of the time, Pallas kernels for 26%

profile of v1, /device:TPU:1, one launch (start us, length us, event | category | flops | bytes accessed | tf_op | source)
XLA Modules:
  0.0 109.0 jit_solution(15421996354501388293)
XLA Ops:
  0.0 1.6 %copy.18 = f32[1,8,16,16,256]{4,3,2,1,0:T(8,128)S(1)} copy(f32[1,8,16,16,256]{4,3,2,1,0:T(8,128)} %param.5) | data formatting | bytes 4194304
  1.6 0.0 copy-start
  1.6 0.1 shard_map.55
  1.7 2.2 %collective-permute-start = (s16[17,16,256]{2,1,0:T(8,128)(2,1)S(1)}, s16[17,16,256]{2,1,0:T(8,128)(2,1)S(1)}, u32[]{:S(2)}, u32[]{:S(2)}) collective-permute-start(s16[17,16,256]{2,1,0:T(8,128)(2,1)S(1)} %get-tuple-element.27), channel_id=1, source_target_pairs={{0,1},{1,0},{2,3},{3,2},{4,5},{5,4},{6,7},{7,6},{8,9},{9,8},{10,11... | collective-permute-start | bytes 417800 | tf_op jit(solution)/shard_map/ppermute | solution.py:523
  3.9 2.2 %collective-permute-start.1 = (s16[17,16,256]{2,1,0:T(8,128)(2,1)S(1)}, s16[17,16,256]{2,1,0:T(8,128)(2,1)S(1)}, u32[]{:S(2)}, u32[]{:S(2)}) collective-permute-start(s16[17,16,256]{2,1,0:T(8,128)(2,1)S(1)} %get-tuple-element.28), channel_id=1, source_target_pairs={{0,3},{1,2},{2,1},{3,0},{4,7},{5,6},{6,5},{7,4},{8,11},{9,10},{10,... | collective-permute-start | bytes 417800 | tf_op jit(solution)/shard_map/ppermute | solution.py:524
  6.1 0.0 copy-done
  6.1 5.9 %shard_map.56 = (f32[8,16,16,256]{3,2,1,0:T(8,128)S(1)}, bf16[6,8,16,16,256]{4,3,2,1,0:T(8,128)(2,1)S(1)}) custom-call(f32[8,16,16,256]{3,2,1,0:T(8,128)S(1)} %get-tuple-element.25.grid, bf16[512,768]{1,0:T(8,128)(2,1)S(1)} %copy-done, bf16[1,6,8,16,16,256]{5,4,3,2,1,0:T(8,128)(2,1)} %velocity.1), custom_call_target="tpu_custom_call" | custom-call | flops 524288000 | bytes 10485760 | tf_op jit(solution)/shard_map/pallas_call | solution.py:198
  12.0 0.0 collective-permute-done.inner
  12.0 0.1 collective-permute-done.1.outer
  12.1 0.3 shard_map.57
  12.4 0.3 collective-permute-start.2
  12.7 2.5 %collective-permute-start.3 = (s16[17,16,256]{2,1,0:T(8,128)(2,1)S(1)}, s16[17,16,256]{2,1,0:T(8,128)(2,1)S(1)}, u32[]{:S(2)}, u32[]{:S(2)}) collective-permute-start(s16[17,16,256]{2,1,0:T(8,128)(2,1)S(1)} %get-tuple-element.32), channel_id=1, source_target_pairs={{0,3},{1,2},{2,1},{3,0},{4,7},{5,6},{6,5},{7,4},{8,11},{9,10},{10,... | collective-permute-start | bytes 417800 | tf_op jit(solution)/shard_map/ppermute | solution.py:524
  15.2 4.3 %shard_map.58.partial = f32[8,16,16,256]{3,2,1,0:T(8,128)S(1)} custom-call(f32[8,16,16,256]{3,2,1,0:T(8,128)S(1)} %get-tuple-element.30.grid, bf16[512,768]{1,0:T(8,128)(2,1)S(1)} %copy-done, bf16[6,8,16,16,256]{4,3,2,1,0:T(8,128)(2,1)S(1)} %get-tuple-element.29.speeds), custom_call_target="tpu_custom_call" | custom-call | flops 524288000 | bytes 10485760 | tf_op jit(solution)/shard_map/pallas_call | solution.py:217
  19.5 0.0 collective-permute-done.2.inner
  19.5 0.5 collective-permute-done.3.outer
  20.1 0.3 shard_map.59
  20.3 0.1 collective-permute-start.4
  20.4 2.6 %collective-permute-start.5 = (s16[17,16,256]{2,1,0:T(8,128)(2,1)S(1)}, s16[17,16,256]{2,1,0:T(8,128)(2,1)S(1)}, u32[]{:S(2)}, u32[]{:S(2)}) collective-permute-start(s16[17,16,256]{2,1,0:T(8,128)(2,1)S(1)} %get-tuple-element.35), channel_id=1, source_target_pairs={{0,3},{1,2},{2,1},{3,0},{4,7},{5,6},{6,5},{7,4},{8,11},{9,10},{10,... | collective-permute-start | bytes 417800 | tf_op jit(solution)/shard_map/ppermute | solution.py:524
  23.0 4.3 %shard_map.60.partial = f32[8,16,16,256]{3,2,1,0:T(8,128)S(1)} custom-call(f32[8,16,16,256]{3,2,1,0:T(8,128)S(1)} %get-tuple-element.33.grid, bf16[512,768]{1,0:T(8,128)(2,1)S(1)} %copy-done, bf16[6,8,16,16,256]{4,3,2,1,0:T(8,128)(2,1)S(1)} %get-tuple-element.29.speeds), custom_call_target="tpu_custom_call" | custom-call | flops 524288000 | bytes 10485760 | tf_op jit(solution)/shard_map/pallas_call | solution.py:217
  27.3 0.0 collective-permute-done.4.inner
  27.3 0.0 collective-permute-done.5.outer
  27.3 0.3 shard_map.61
  27.6 0.6 collective-permute-start.6
  28.2 2.6 %collective-permute-start.7 = (s16[17,16,256]{2,1,0:T(8,128)(2,1)S(1)}, s16[17,16,256]{2,1,0:T(8,128)(2,1)S(1)}, u32[]{:S(2)}, u32[]{:S(2)}) collective-permute-start(s16[17,16,256]{2,1,0:T(8,128)(2,1)S(1)} %get-tuple-element.38), channel_id=1, source_target_pairs={{0,3},{1,2},{2,1},{3,0},{4,7},{5,6},{6,5},{7,4},{8,11},{9,10},{10,... | collective-permute-start | bytes 417800 | tf_op jit(solution)/shard_map/ppermute | solution.py:524
  30.7 4.3 %shard_map.62.partial = f32[8,16,16,256]{3,2,1,0:T(8,128)S(1)} custom-call(f32[8,16,16,256]{3,2,1,0:T(8,128)S(1)} %get-tuple-element.36.grid, bf16[512,768]{1,0:T(8,128)(2,1)S(1)} %copy-done, bf16[6,8,16,16,256]{4,3,2,1,0:T(8,128)(2,1)S(1)} %get-tuple-element.29.speeds), custom_call_target="tpu_custom_call" | custom-call | flops 524288000 | bytes 10485760 | tf_op jit(solution)/shard_map/pallas_call | solution.py:217
  35.0 0.0 collective-permute-done.6.inner
  35.0 0.0 collective-permute-done.7.outer
  35.0 0.5 shard_map.63
  35.6 0.0 copy-start.1
  35.6 1.0 copy-done.1
  36.6 0.0 copy-start.4
  36.6 0.0 copy-start.3
  36.6 8.1 %all-to-all-start = ((s16[32,136,128]{2,1,0:T(8,128)(2,1)}), s16[32,136,128]{2,1,0:T(8,128)(2,1)S(1)}, u32[]{:S(2)}, u32[]{:S(2)}) async-start(s16[32,136,128]{2,1,0:T(8,128)(2,1)} %copy-done.1), calls=%async_computation | async-start | bytes 2228224 | tf_op jit(solution)/shard_map/all_to_all | solution.py:534
  44.8 0.0 copy-done.4
  44.8 0.8 copy.11.owners
  45.5 9.9 %shard_map.64.table = s32[8,24]{1,0:T(8,128)} custom-call(s32[196,8]{1,0:T(8,128)} %copy.11.owners), custom_call_target="tpu_custom_call" | custom-call | tf_op jit(solution)/shard_map/pallas_call | solution.py:505
  55.4 17.1 %all-to-all-done.columns = s16[32,136,128]{2,1,0:T(8,128)(2,1)S(1)} async-done(((s16[32,136,128]{2,1,0:T(8,128)(2,1)}), s16[32,136,128]{2,1,0:T(8,128)(2,1)S(1)}, u32[]{:S(2)}, u32[]{:S(2)}) %all-to-all-start) | async-done | bytes 1114144 | tf_op jit(solution)/shard_map/all_to_all | solution.py:534
  72.5 0.0 copy-done.3
  72.5 0.0 copy-start.2
  72.5 0.7 copy-done.2
  73.2 3.5 %shard_map.65 = s16[32,136,128]{2,1,0:T(8,128)(2,1)} custom-call(s32[8,24]{1,0:T(8,128)S(1)} %copy-done.2, s32[8]{0:T(128)S(1)} %copy-done.3, s16[32,136,128]{2,1,0:T(8,128)(2,1)S(1)} %all-to-all-done.columns), custom_call_target="tpu_custom_call" | custom-call | tf_op jit(solution)/shard_map/pallas_call | solution.py:415
  76.7 3.2 %all-to-all-start.1 = ((s16[32,136,128]{2,1,0:T(8,128)(2,1)}), s16[32,136,128]{2,1,0:T(8,128)(2,1)S(1)}, u32[]{:S(2)}, u32[]{:S(2)}) async-start(s16[32,136,128]{2,1,0:T(8,128)(2,1)} %shard_map.65), calls=%async_computation.1 | async-start | bytes 2228224 | tf_op jit(solution)/shard_map/all_to_all | solution.py:539
  79.8 0.6 dynamic_slice.3
  81.1 26.5 %all-to-all-done.1.changes = s16[32,136,128]{2,1,0:T(8,128)(2,1)S(1)} async-done(((s16[32,136,128]{2,1,0:T(8,128)(2,1)}), s16[32,136,128]{2,1,0:T(8,128)(2,1)S(1)}, u32[]{:S(2)}, u32[]{:S(2)}) %all-to-all-start.1) | async-done | bytes 1114144 | tf_op jit(solution)/shard_map/all_to_all | solution.py:539
  107.6 1.4 %shard_map.66 = f32[1,8,16,16,256]{4,3,2,1,0:T(8,128)} custom-call(f32[1]{0:T(128)S(6)} %convert_element_type.3.weight, f32[8,16,16,256]{3,2,1,0:T(8,128)S(1)} %get-tuple-element.43.grid, s16[32,136,128]{2,1,0:T(8,128)(2,1)S(1)} %all-to-all-done.1.changes), custom_call_target="tpu_custom_call" | custom-call | tf_op jit(solution)/shard_map/pallas_call | solution.py:451
Async XLA Ops:
  1.6 4.5 %copy-start = (bf16[512,768]{1,0:T(8,128)(2,1)S(1)}, bf16[512,768]{1,0:T(8,128)(2,1)}, u32[]{:S(2)}) copy-start(bf16[512,768]{1,0:T(8,128)(2,1)} %constant.27.clone.matrix) | copy-start | bytes 2359300
  1.7 10.3 %collective-permute-start = (s16[17,16,256]{2,1,0:T(8,128)(2,1)S(1)}, s16[17,16,256]{2,1,0:T(8,128)(2,1)S(1)}, u32[]{:S(2)}, u32[]{:S(2)}) collective-permute-start(s16[17,16,256]{2,1,0:T(8,128)(2,1)S(1)} %get-tuple-element.27), channel_id=1, source_target_pairs={{0,1},{1,0},{2,3},{3,2},{4,5},{5,4},{6,7},{7,6},{8,9},{9,8},{10,11... | collective-permute-start | bytes 417800 | tf_op jit(solution)/shard_map/ppermute | solution.py:523
  3.9 8.3 %collective-permute-start.1 = (s16[17,16,256]{2,1,0:T(8,128)(2,1)S(1)}, s16[17,16,256]{2,1,0:T(8,128)(2,1)S(1)}, u32[]{:S(2)}, u32[]{:S(2)}) collective-permute-start(s16[17,16,256]{2,1,0:T(8,128)(2,1)S(1)} %get-tuple-element.28), channel_id=1, source_target_pairs={{0,3},{1,2},{2,1},{3,0},{4,7},{5,6},{6,5},{7,4},{8,11},{9,10},{10,... | collective-permute-start | bytes 417800 | tf_op jit(solution)/shard_map/ppermute | solution.py:524
  12.4 7.1 %collective-permute-start.2 = (s16[17,16,256]{2,1,0:T(8,128)(2,1)S(1)}, s16[17,16,256]{2,1,0:T(8,128)(2,1)S(1)}, u32[]{:S(2)}, u32[]{:S(2)}) collective-permute-start(s16[17,16,256]{2,1,0:T(8,128)(2,1)S(1)} %get-tuple-element.31), channel_id=1, source_target_pairs={{0,1},{1,0},{2,3},{3,2},{4,5},{5,4},{6,7},{7,6},{8,9},{9,8},{10,11... | collective-permute-start | bytes 417800 | tf_op jit(solution)/shard_map/ppermute | solution.py:523
  12.7 7.3 %collective-permute-start.3 = (s16[17,16,256]{2,1,0:T(8,128)(2,1)S(1)}, s16[17,16,256]{2,1,0:T(8,128)(2,1)S(1)}, u32[]{:S(2)}, u32[]{:S(2)}) collective-permute-start(s16[17,16,256]{2,1,0:T(8,128)(2,1)S(1)} %get-tuple-element.32), channel_id=1, source_target_pairs={{0,3},{1,2},{2,1},{3,0},{4,7},{5,6},{6,5},{7,4},{8,11},{9,10},{10,... | collective-permute-start | bytes 417800 | tf_op jit(solution)/shard_map/ppermute | solution.py:524
  20.3 7.0 %collective-permute-start.4 = (s16[17,16,256]{2,1,0:T(8,128)(2,1)S(1)}, s16[17,16,256]{2,1,0:T(8,128)(2,1)S(1)}, u32[]{:S(2)}, u32[]{:S(2)}) collective-permute-start(s16[17,16,256]{2,1,0:T(8,128)(2,1)S(1)} %get-tuple-element.34), channel_id=1, source_target_pairs={{0,1},{1,0},{2,3},{3,2},{4,5},{5,4},{6,7},{7,6},{8,9},{9,8},{10,11... | collective-permute-start | bytes 417800 | tf_op jit(solution)/shard_map/ppermute | solution.py:523
  20.4 6.9 %collective-permute-start.5 = (s16[17,16,256]{2,1,0:T(8,128)(2,1)S(1)}, s16[17,16,256]{2,1,0:T(8,128)(2,1)S(1)}, u32[]{:S(2)}, u32[]{:S(2)}) collective-permute-start(s16[17,16,256]{2,1,0:T(8,128)(2,1)S(1)} %get-tuple-element.35), channel_id=1, source_target_pairs={{0,3},{1,2},{2,1},{3,0},{4,7},{5,6},{6,5},{7,4},{8,11},{9,10},{10,... | collective-permute-start | bytes 417800 | tf_op jit(solution)/shard_map/ppermute | solution.py:524
  27.6 7.4 %collective-permute-start.6 = (s16[17,16,256]{2,1,0:T(8,128)(2,1)S(1)}, s16[17,16,256]{2,1,0:T(8,128)(2,1)S(1)}, u32[]{:S(2)}, u32[]{:S(2)}) collective-permute-start(s16[17,16,256]{2,1,0:T(8,128)(2,1)S(1)} %get-tuple-element.37), channel_id=1, source_target_pairs={{0,1},{1,0},{2,3},{3,2},{4,5},{5,4},{6,7},{7,6},{8,9},{9,8},{10,11... | collective-permute-start | bytes 417800 | tf_op jit(solution)/shard_map/ppermute | solution.py:523
  28.2 6.9 %collective-permute-start.7 = (s16[17,16,256]{2,1,0:T(8,128)(2,1)S(1)}, s16[17,16,256]{2,1,0:T(8,128)(2,1)S(1)}, u32[]{:S(2)}, u32[]{:S(2)}) collective-permute-start(s16[17,16,256]{2,1,0:T(8,128)(2,1)S(1)} %get-tuple-element.38), channel_id=1, source_target_pairs={{0,3},{1,2},{2,1},{3,0},{4,7},{5,6},{6,5},{7,4},{8,11},{9,10},{10,... | collective-permute-start | bytes 417800 | tf_op jit(solution)/shard_map/ppermute | solution.py:524
  35.6 1.0 copy-start.1
  36.6 8.2 %copy-start.4 = (s32[196,8]{0,1:T(8,128)S(1)}, s32[196,8]{0,1:T(8,128)}, u32[]{:S(2)}) copy-start(s32[196,8]{0,1:T(8,128)} %param.8) | copy-start | bytes 18820
  36.6 35.9 %copy-start.3 = (s32[8]{0:T(128)S(1)}, s32[8]{0:T(128)}, u32[]{:S(2)}) copy-start(s32[8]{0:T(128)} %weights.1) | copy-start | bytes 100
  36.6 35.9 %all-to-all-start = ((s16[32,136,128]{2,1,0:T(8,128)(2,1)}), s16[32,136,128]{2,1,0:T(8,128)(2,1)S(1)}, u32[]{:S(2)}, u32[]{:S(2)}) async-start(s16[32,136,128]{2,1,0:T(8,128)(2,1)} %copy-done.1), calls=%async_computation | async-start | bytes 2228224 | tf_op jit(solution)/shard_map/all_to_all | solution.py:534
  72.5 0.7 copy-start.2
  76.7 30.9 %all-to-all-start.1 = ((s16[32,136,128]{2,1,0:T(8,128)(2,1)}), s16[32,136,128]{2,1,0:T(8,128)(2,1)S(1)}, u32[]{:S(2)}, u32[]{:S(2)}) async-start(s16[32,136,128]{2,1,0:T(8,128)(2,1)} %shard_map.65), calls=%async_computation.1 | async-start | bytes 2228224 | tf_op jit(solution)/shard_map/all_to_all | solution.py:539

commit v2 on v1

--- a/solution.py
+++ b/solution.py
@@ -358,7 +358,7 @@
             values[source * cut.planes + plane] = value
         return carry
 
-    lax.fori_loop(0, cut.count, unpack, 0, unroll=2)
+    lax.fori_loop(0, cut.count, unpack, 0, unroll=4)
 
     def gather(comp, carry):
         weight = weights[comp].astype(jnp.float32)
@@ -374,7 +374,7 @@
             rows[comp * MULTI + index] = values[base + slab] * weight + near * share
         return carry
 
-    lax.fori_loop(0, comp_count, gather, 0)
+    lax.fori_loop(0, comp_count, gather, 0, unroll=2)
     for index in range(SHARED):
         total = rows[index]
         for comp in range(1, comp_count):
@@ -406,7 +406,7 @@
             cut.put(out, comp * dom_count + dom, lambda p: nodal[dom * cut.planes + p])
         return carry
 
-    lax.fori_loop(0, comp_count, send, 0)
+    lax.fori_loop(0, comp_count, send, 0, unroll=2)
 
 
 def merge_columns(cut, columns, table, weights, dom_count):

time: 109 us -> 109 us (level)
  no operation moved by 1% of the time
where the time goes in v2:
time: 109 us
  waiting for transfers between devices  44.3 us (41%)
  Pallas kernels  34.8 us (32%)
  starting transfers between devices  24.3 us (22%)
  local copies, waits for them, and re-layouts  4.65 us (4%)
    all_to_all x1, waiting for transfers between devices, local(): changes = lax.all_to_all(changes, ('comp', 'dom'), 0, 0, tiled=True)  26.5 us
    all_to_all x1, waiting for transfers between devices, local(): columns = lax.all_to_all(columns, ('comp', 'dom'), 0, 0, tiled=True)  17.1 us
    pallas_call x3, Pallas kernels, advance_planes(): pl.pallas_call(advance_body, in_specs=[vmem()] * 3, out_specs=vmem(), out...  12.9 us
    ppermute x4, starting transfers between devices, local(): outer = lax.ppermute(to_outer, 'dom', outer_pairs)  9.87 us
    pallas_call x1, Pallas kernels, merge_tables(): pl.pallas_call(tables_body, in_specs=[smem()], out_specs=smem(), out_shap...  9.86 us
    all_to_all x1, starting transfers between devices, local(): columns = lax.all_to_all(columns, ('comp', 'dom'), 0, 0, tiled=True)  8.15 us
    pallas_call x1, Pallas kernels, first_planes(): pl.pallas_call(first_body, in_specs=[vmem(), vmem(), hbm()], out_specs=[v...  5.9 us
    pallas_call x1, Pallas kernels, merge_columns(): pl.pallas_call(functools.partial(merge_body, cut, dom_count), in_specs=[s...  3.34 us
  transfers between devices with their start and end apart: 10, of which 4 were waited for; matrix products, arithmetic and copies ran while one was open for 1% of the time, Pallas kernels for 26%

profile of v2, /device:TPU:1, one launch (start us, length us, event | category | flops | bytes accessed | tf_op | source)
XLA Modules:
  0.0 108.9 jit_solution(7340934712818224247)
XLA Ops:
  0.0 1.6 %copy.18 = f32[1,8,16,16,256]{4,3,2,1,0:T(8,128)S(1)} copy(f32[1,8,16,16,256]{4,3,2,1,0:T(8,128)} %param.5) | data formatting | bytes 4194304
  1.6 0.0 copy-start
  1.6 0.1 shard_map.55
  1.7 2.2 %collective-permute-start = (s16[17,16,256]{2,1,0:T(8,128)(2,1)S(1)}, s16[17,16,256]{2,1,0:T(8,128)(2,1)S(1)}, u32[]{:S(2)}, u32[]{:S(2)}) collective-permute-start(s16[17,16,256]{2,1,0:T(8,128)(2,1)S(1)} %get-tuple-element.27), channel_id=1, source_target_pairs={{0,1},{1,0},{2,3},{3,2},{4,5},{5,4},{6,7},{7,6},{8,9},{9,8},{10,11... | collective-permute-start | bytes 417800 | tf_op jit(solution)/shard_map/ppermute | solution.py:523
  3.9 2.2 %collective-permute-start.1 = (s16[17,16,256]{2,1,0:T(8,128)(2,1)S(1)}, s16[17,16,256]{2,1,0:T(8,128)(2,1)S(1)}, u32[]{:S(2)}, u32[]{:S(2)}) collective-permute-start(s16[17,16,256]{2,1,0:T(8,128)(2,1)S(1)} %get-tuple-element.28), channel_id=1, source_target_pairs={{0,3},{1,2},{2,1},{3,0},{4,7},{5,6},{6,5},{7,4},{8,11},{9,10},{10,... | collective-permute-start | bytes 417800 | tf_op jit(solution)/shard_map/ppermute | solution.py:524
  6.1 0.0 copy-done
  6.1 5.9 %shard_map.56 = (f32[8,16,16,256]{3,2,1,0:T(8,128)S(1)}, bf16[6,8,16,16,256]{4,3,2,1,0:T(8,128)(2,1)S(1)}) custom-call(f32[8,16,16,256]{3,2,1,0:T(8,128)S(1)} %get-tuple-element.25.grid, bf16[512,768]{1,0:T(8,128)(2,1)S(1)} %copy-done, bf16[1,6,8,16,16,256]{5,4,3,2,1,0:T(8,128)(2,1)} %velocity.1), custom_call_target="tpu_custom_call" | custom-call | flops 524288000 | bytes 10485760 | tf_op jit(solution)/shard_map/pallas_call | solution.py:198
  12.0 0.0 collective-permute-done.inner
  12.0 0.1 collective-permute-done.1.outer
  12.1 0.3 shard_map.57
  12.4 0.3 collective-permute-start.2
  12.7 2.5 %collective-permute-start.3 = (s16[17,16,256]{2,1,0:T(8,128)(2,1)S(1)}, s16[17,16,256]{2,1,0:T(8,128)(2,1)S(1)}, u32[]{:S(2)}, u32[]{:S(2)}) collective-permute-start(s16[17,16,256]{2,1,0:T(8,128)(2,1)S(1)} %get-tuple-element.32), channel_id=1, source_target_pairs={{0,3},{1,2},{2,1},{3,0},{4,7},{5,6},{6,5},{7,4},{8,11},{9,10},{10,... | collective-permute-start | bytes 417800 | tf_op jit(solution)/shard_map/ppermute | solution.py:524
  15.2 4.3 %shard_map.58.partial = f32[8,16,16,256]{3,2,1,0:T(8,128)S(1)} custom-call(f32[8,16,16,256]{3,2,1,0:T(8,128)S(1)} %get-tuple-element.30.grid, bf16[512,768]{1,0:T(8,128)(2,1)S(1)} %copy-done, bf16[6,8,16,16,256]{4,3,2,1,0:T(8,128)(2,1)S(1)} %get-tuple-element.29.speeds), custom_call_target="tpu_custom_call" | custom-call | flops 524288000 | bytes 10485760 | tf_op jit(solution)/shard_map/pallas_call | solution.py:217
  19.5 0.0 collective-permute-done.2.inner
  19.5 0.5 collective-permute-done.3.outer
  20.1 0.3 shard_map.59
  20.3 0.1 collective-permute-start.4
  20.4 2.6 %collective-permute-start.5 = (s16[17,16,256]{2,1,0:T(8,128)(2,1)S(1)}, s16[17,16,256]{2,1,0:T(8,128)(2,1)S(1)}, u32[]{:S(2)}, u32[]{:S(2)}) collective-permute-start(s16[17,16,256]{2,1,0:T(8,128)(2,1)S(1)} %get-tuple-element.35), channel_id=1, source_target_pairs={{0,3},{1,2},{2,1},{3,0},{4,7},{5,6},{6,5},{7,4},{8,11},{9,10},{10,... | collective-permute-start | bytes 417800 | tf_op jit(solution)/shard_map/ppermute | solution.py:524
  23.0 4.3 %shard_map.60.partial = f32[8,16,16,256]{3,2,1,0:T(8,128)S(1)} custom-call(f32[8,16,16,256]{3,2,1,0:T(8,128)S(1)} %get-tuple-element.33.grid, bf16[512,768]{1,0:T(8,128)(2,1)S(1)} %copy-done, bf16[6,8,16,16,256]{4,3,2,1,0:T(8,128)(2,1)S(1)} %get-tuple-element.29.speeds), custom_call_target="tpu_custom_call" | custom-call | flops 524288000 | bytes 10485760 | tf_op jit(solution)/shard_map/pallas_call | solution.py:217
  27.3 0.0 collective-permute-done.4.inner
  27.3 0.0 collective-permute-done.5.outer
  27.3 0.3 shard_map.61
  27.6 0.6 collective-permute-start.6
  28.2 2.6 %collective-permute-start.7 = (s16[17,16,256]{2,1,0:T(8,128)(2,1)S(1)}, s16[17,16,256]{2,1,0:T(8,128)(2,1)S(1)}, u32[]{:S(2)}, u32[]{:S(2)}) collective-permute-start(s16[17,16,256]{2,1,0:T(8,128)(2,1)S(1)} %get-tuple-element.38), channel_id=1, source_target_pairs={{0,3},{1,2},{2,1},{3,0},{4,7},{5,6},{6,5},{7,4},{8,11},{9,10},{10,... | collective-permute-start | bytes 417800 | tf_op jit(solution)/shard_map/ppermute | solution.py:524
  30.7 4.3 %shard_map.62.partial = f32[8,16,16,256]{3,2,1,0:T(8,128)S(1)} custom-call(f32[8,16,16,256]{3,2,1,0:T(8,128)S(1)} %get-tuple-element.36.grid, bf16[512,768]{1,0:T(8,128)(2,1)S(1)} %copy-done, bf16[6,8,16,16,256]{4,3,2,1,0:T(8,128)(2,1)S(1)} %get-tuple-element.29.speeds), custom_call_target="tpu_custom_call" | custom-call | flops 524288000 | bytes 10485760 | tf_op jit(solution)/shard_map/pallas_call | solution.py:217
  35.0 0.0 collective-permute-done.6.inner
  35.0 0.0 collective-permute-done.7.outer
  35.0 0.5 shard_map.63
  35.6 0.0 copy-start.1
  35.6 1.0 copy-done.1
  36.6 0.0 copy-start.4
  36.6 0.0 copy-start.3
  36.6 8.1 %all-to-all-start = ((s16[32,136,128]{2,1,0:T(8,128)(2,1)}), s16[32,136,128]{2,1,0:T(8,128)(2,1)S(1)}, u32[]{:S(2)}, u32[]{:S(2)}) async-start(s16[32,136,128]{2,1,0:T(8,128)(2,1)} %copy-done.1), calls=%async_computation | async-start | bytes 2228224 | tf_op jit(solution)/shard_map/all_to_all | solution.py:534
  44.8 0.0 copy-done.4
  44.8 0.8 copy.11.owners
  45.5 9.9 %shard_map.64.table = s32[8,24]{1,0:T(8,128)} custom-call(s32[196,8]{1,0:T(8,128)} %copy.11.owners), custom_call_target="tpu_custom_call" | custom-call | tf_op jit(solution)/shard_map/pallas_call | solution.py:505
  55.4 17.1 %all-to-all-done.columns = s16[32,136,128]{2,1,0:T(8,128)(2,1)S(1)} async-done(((s16[32,136,128]{2,1,0:T(8,128)(2,1)}), s16[32,136,128]{2,1,0:T(8,128)(2,1)S(1)}, u32[]{:S(2)}, u32[]{:S(2)}) %all-to-all-start) | async-done | bytes 1114144 | tf_op jit(solution)/shard_map/all_to_all | solution.py:534
  72.5 0.0 copy-done.3
  72.5 0.0 copy-start.2
  72.5 0.7 copy-done.2
  73.2 3.3 %shard_map.65 = s16[32,136,128]{2,1,0:T(8,128)(2,1)} custom-call(s32[8,24]{1,0:T(8,128)S(1)} %copy-done.2, s32[8]{0:T(128)S(1)} %copy-done.3, s16[32,136,128]{2,1,0:T(8,128)(2,1)S(1)} %all-to-all-done.columns), custom_call_target="tpu_custom_call" | custom-call | tf_op jit(solution)/shard_map/pallas_call | solution.py:415
  76.5 3.2 %all-to-all-start.1 = ((s16[32,136,128]{2,1,0:T(8,128)(2,1)}), s16[32,136,128]{2,1,0:T(8,128)(2,1)S(1)}, u32[]{:S(2)}, u32[]{:S(2)}) async-start(s16[32,136,128]{2,1,0:T(8,128)(2,1)} %shard_map.65), calls=%async_computation.1 | async-start | bytes 2228224 | tf_op jit(solution)/shard_map/all_to_all | solution.py:539
  79.7 0.6 dynamic_slice.3
  80.9 26.5 %all-to-all-done.1.changes = s16[32,136,128]{2,1,0:T(8,128)(2,1)S(1)} async-done(((s16[32,136,128]{2,1,0:T(8,128)(2,1)}), s16[32,136,128]{2,1,0:T(8,128)(2,1)S(1)}, u32[]{:S(2)}, u32[]{:S(2)}) %all-to-all-start.1) | async-done | bytes 1114144 | tf_op jit(solution)/shard_map/all_to_all | solution.py:539
  107.4 1.4 %shard_map.66 = f32[1,8,16,16,256]{4,3,2,1,0:T(8,128)} custom-call(f32[1]{0:T(128)S(6)} %convert_element_type.3.weight, f32[8,16,16,256]{3,2,1,0:T(8,128)S(1)} %get-tuple-element.43.grid, s16[32,136,128]{2,1,0:T(8,128)(2,1)S(1)} %all-to-all-done.1.changes), custom_call_target="tpu_custom_call" | custom-call | tf_op jit(solution)/shard_map/pallas_call | solution.py:451
Async XLA Ops:
  1.6 4.5 %copy-start = (bf16[512,768]{1,0:T(8,128)(2,1)S(1)}, bf16[512,768]{1,0:T(8,128)(2,1)}, u32[]{:S(2)}) copy-start(bf16[512,768]{1,0:T(8,128)(2,1)} %constant.27.clone.matrix) | copy-start | bytes 2359300
  1.7 10.3 %collective-permute-start = (s16[17,16,256]{2,1,0:T(8,128)(2,1)S(1)}, s16[17,16,256]{2,1,0:T(8,128)(2,1)S(1)}, u32[]{:S(2)}, u32[]{:S(2)}) collective-permute-start(s16[17,16,256]{2,1,0:T(8,128)(2,1)S(1)} %get-tuple-element.27), channel_id=1, source_target_pairs={{0,1},{1,0},{2,3},{3,2},{4,5},{5,4},{6,7},{7,6},{8,9},{9,8},{10,11... | collective-permute-start | bytes 417800 | tf_op jit(solution)/shard_map/ppermute | solution.py:523
  3.9 8.3 %collective-permute-start.1 = (s16[17,16,256]{2,1,0:T(8,128)(2,1)S(1)}, s16[17,16,256]{2,1,0:T(8,128)(2,1)S(1)}, u32[]{:S(2)}, u32[]{:S(2)}) collective-permute-start(s16[17,16,256]{2,1,0:T(8,128)(2,1)S(1)} %get-tuple-element.28), channel_id=1, source_target_pairs={{0,3},{1,2},{2,1},{3,0},{4,7},{5,6},{6,5},{7,4},{8,11},{9,10},{10,... | collective-permute-start | bytes 417800 | tf_op jit(solution)/shard_map/ppermute | solution.py:524
  12.4 7.1 %collective-permute-start.2 = (s16[17,16,256]{2,1,0:T(8,128)(2,1)S(1)}, s16[17,16,256]{2,1,0:T(8,128)(2,1)S(1)}, u32[]{:S(2)}, u32[]{:S(2)}) collective-permute-start(s16[17,16,256]{2,1,0:T(8,128)(2,1)S(1)} %get-tuple-element.31), channel_id=1, source_target_pairs={{0,1},{1,0},{2,3},{3,2},{4,5},{5,4},{6,7},{7,6},{8,9},{9,8},{10,11... | collective-permute-start | bytes 417800 | tf_op jit(solution)/shard_map/ppermute | solution.py:523
  12.7 7.3 %collective-permute-start.3 = (s16[17,16,256]{2,1,0:T(8,128)(2,1)S(1)}, s16[17,16,256]{2,1,0:T(8,128)(2,1)S(1)}, u32[]{:S(2)}, u32[]{:S(2)}) collective-permute-start(s16[17,16,256]{2,1,0:T(8,128)(2,1)S(1)} %get-tuple-element.32), channel_id=1, source_target_pairs={{0,3},{1,2},{2,1},{3,0},{4,7},{5,6},{6,5},{7,4},{8,11},{9,10},{10,... | collective-permute-start | bytes 417800 | tf_op jit(solution)/shard_map/ppermute | solution.py:524
  20.3 7.0 %collective-permute-start.4 = (s16[17,16,256]{2,1,0:T(8,128)(2,1)S(1)}, s16[17,16,256]{2,1,0:T(8,128)(2,1)S(1)}, u32[]{:S(2)}, u32[]{:S(2)}) collective-permute-start(s16[17,16,256]{2,1,0:T(8,128)(2,1)S(1)} %get-tuple-element.34), channel_id=1, source_target_pairs={{0,1},{1,0},{2,3},{3,2},{4,5},{5,4},{6,7},{7,6},{8,9},{9,8},{10,11... | collective-permute-start | bytes 417800 | tf_op jit(solution)/shard_map/ppermute | solution.py:523
  20.4 6.9 %collective-permute-start.5 = (s16[17,16,256]{2,1,0:T(8,128)(2,1)S(1)}, s16[17,16,256]{2,1,0:T(8,128)(2,1)S(1)}, u32[]{:S(2)}, u32[]{:S(2)}) collective-permute-start(s16[17,16,256]{2,1,0:T(8,128)(2,1)S(1)} %get-tuple-element.35), channel_id=1, source_target_pairs={{0,3},{1,2},{2,1},{3,0},{4,7},{5,6},{6,5},{7,4},{8,11},{9,10},{10,... | collective-permute-start | bytes 417800 | tf_op jit(solution)/shard_map/ppermute | solution.py:524
  27.6 7.4 %collective-permute-start.6 = (s16[17,16,256]{2,1,0:T(8,128)(2,1)S(1)}, s16[17,16,256]{2,1,0:T(8,128)(2,1)S(1)}, u32[]{:S(2)}, u32[]{:S(2)}) collective-permute-start(s16[17,16,256]{2,1,0:T(8,128)(2,1)S(1)} %get-tuple-element.37), channel_id=1, source_target_pairs={{0,1},{1,0},{2,3},{3,2},{4,5},{5,4},{6,7},{7,6},{8,9},{9,8},{10,11... | collective-permute-start | bytes 417800 | tf_op jit(solution)/shard_map/ppermute | solution.py:523
  28.2 6.9 %collective-permute-start.7 = (s16[17,16,256]{2,1,0:T(8,128)(2,1)S(1)}, s16[17,16,256]{2,1,0:T(8,128)(2,1)S(1)}, u32[]{:S(2)}, u32[]{:S(2)}) collective-permute-start(s16[17,16,256]{2,1,0:T(8,128)(2,1)S(1)} %get-tuple-element.38), channel_id=1, source_target_pairs={{0,3},{1,2},{2,1},{3,0},{4,7},{5,6},{6,5},{7,4},{8,11},{9,10},{10,... | collective-permute-start | bytes 417800 | tf_op jit(solution)/shard_map/ppermute | solution.py:524
  35.6 1.0 copy-start.1
  36.6 8.2 %copy-start.4 = (s32[196,8]{0,1:T(8,128)S(1)}, s32[196,8]{0,1:T(8,128)}, u32[]{:S(2)}) copy-start(s32[196,8]{0,1:T(8,128)} %param.8) | copy-start | bytes 18820
  36.6 35.9 %copy-start.3 = (s32[8]{0:T(128)S(1)}, s32[8]{0:T(128)}, u32[]{:S(2)}) copy-start(s32[8]{0:T(128)} %weights.1) | copy-start | bytes 100
  36.6 35.9 %all-to-all-start = ((s16[32,136,128]{2,1,0:T(8,128)(2,1)}), s16[32,136,128]{2,1,0:T(8,128)(2,1)S(1)}, u32[]{:S(2)}, u32[]{:S(2)}) async-start(s16[32,136,128]{2,1,0:T(8,128)(2,1)} %copy-done.1), calls=%async_computation | async-start | bytes 2228224 | tf_op jit(solution)/shard_map/all_to_all | solution.py:534
  72.5 0.7 copy-start.2
  76.5 30.9 %all-to-all-start.1 = ((s16[32,136,128]{2,1,0:T(8,128)(2,1)}), s16[32,136,128]{2,1,0:T(8,128)(2,1)S(1)}, u32[]{:S(2)}, u32[]{:S(2)}) async-start(s16[32,136,128]{2,1,0:T(8,128)(2,1)} %shard_map.65), calls=%async_computation.1 | async-start | bytes 2228224 | tf_op jit(solution)/shard_map/all_to_all | solution.py:539
